TPU v7x, 32 devices: a whole 2x2x4 slice. The times are simulated.
32 devices in a mesh: var: 4 (over y, x), dp: 8 (over z, core).
Axes of the slice: x: 2, y: 2, z: 4, core: 2. Of those that a mesh axis runs over, the one named last changes fastest.
Arguments:
- fields: bfloat16 [8, 16, 32, 128], P('dp', 'var'), may hold values from -6 to 6
- kernels: bfloat16 [16, 16, 512], P('var'), may hold values from -1.5 to 1.5
- level_map: int32 [16], P('var'), may hold values 0 or 1
- norm_gain_vector: float32 [512], replicated, may hold values from 0.1 to 1.9
- w_in: bfloat16 [512, 2048], replicated, may hold values from -0.25 to 0.25
- w_out: bfloat16 [2048, 512], replicated, may hold values from -0.125 to 0.125
- cotangent: bfloat16 [8, 4, 256, 512], P('dp', None, 'var'), may hold values from -6 to 6
Outputs:
- block_out: bfloat16 [8, 4, 256, 512], P('dp', None, 'var')
- kernel_grad: float32 [16, 16, 512], P('var', None, 'dp')
Inputs may be any that keep to these rules, and one draw needn't show every extreme that they name: variable-level v belongs to pressure level v // 4 and enters its aggregate where level_map[v] is 1.
All inputs are finite; a program needn't handle non-finite values. No bound on the sum of `level_map` on one device may be relied on, other than what follows from the above.
Results may differ from a plain program's by a relative error of at most 0.013.
Values may be sent and summed in bfloat16 or wider, within the bound.
A program may use at most 64 MiB of HBM per device.

v0:
```python
import jax
import jax.numpy as jnp
from jax import lax
from jax.sharding import PartitionSpec as P

PATCH = 4


def patches_of(images):
    batch, count_v, height, width = images.shape
    shaped = images.reshape(batch, count_v, height // PATCH, PATCH, width // PATCH, PATCH)
    return shaped.transpose(0, 1, 2, 4, 3, 5).reshape(
        batch, count_v, height // PATCH * (width // PATCH), PATCH * PATCH
    )


def block_pass(token_rows, grads, norm_gain_vector, w_in, w_out):
    width = token_rows.shape[-1]
    rows = token_rows.reshape(-1, width).astype(jnp.float32)
    mean_row = jnp.mean(rows, axis=1, keepdims=True)
    centered_rows = rows - mean_row
    reciprocal_std = lax.rsqrt(
        jnp.mean(centered_rows * centered_rows, axis=1, keepdims=True) + 1e-05
    )
    normalized_input = centered_rows * reciprocal_std
    normalized_rows = (normalized_input * norm_gain_vector).astype(jnp.bfloat16)
    pre = jnp.dot(normalized_rows, w_in, preferred_element_type=jnp.float32)
    hidden = jax.nn.gelu(pre, approximate=True).astype(jnp.bfloat16)
    output = (rows + jnp.dot(hidden, w_out, preferred_element_type=jnp.float32)).astype(
        jnp.bfloat16
    )
    gradient_rows = grads.reshape(-1, width)
    dhid = jnp.dot(gradient_rows, w_out.T, preferred_element_type=jnp.float32)
    gelu_back = jax.vjp(lambda value: jax.nn.gelu(value, approximate=True), pre)[1]
    dpre = gelu_back(dhid)[0].astype(jnp.bfloat16)
    dnorm = jnp.dot(dpre, w_in.T, preferred_element_type=jnp.float32)
    normalized_gradient = dnorm * norm_gain_vector
    token_gradient = gradient_rows.astype(jnp.float32) + reciprocal_std * (
        normalized_gradient
        - jnp.mean(normalized_gradient, axis=1, keepdims=True)
        - normalized_input * jnp.mean(normalized_gradient * normalized_input, axis=1, keepdims=True)
    )
    return (
        output.reshape(token_rows.shape),
        token_gradient.astype(jnp.bfloat16).reshape(token_rows.shape),
    )


def level_tables(level, weight, groups):
    onehot = (level[None, :] == jnp.arange(groups, dtype=jnp.int32)[:, None]).astype(
        jnp.float32
    ) * weight[None, :]
    inv = 1.0 / jnp.maximum(jnp.sum(onehot, axis=1), 1.0)
    return (onehot * inv[:, None], inv[level] * weight)


def local(fields, kernels, level_map, norm_gain_vector, w_in, w_out, cotangent):
    batch, var_local = (fields.shape[0], fields.shape[1])
    patch_inputs = patches_of(fields)
    tokens_all = patch_inputs.shape[2]
    scale = float(batch * lax.axis_size("dp") * tokens_all) ** (-0.5)
    own_level = jnp.zeros((var_local,), jnp.int32)
    own_assign, own_member = level_tables(own_level, level_map.astype(jnp.float32), 1)
    patch_embeddings = jnp.einsum(
        "bvnp,vpe->bvne", patch_inputs, kernels, preferred_element_type=jnp.float32
    )
    token_rows = jnp.einsum("lv,bvne->blne", own_assign, patch_embeddings).astype(jnp.bfloat16)
    row_tokens = lax.all_to_all(token_rows, "var", split_axis=2, concat_axis=1, tiled=True)
    block_out, token_gradient = block_pass(row_tokens, cotangent, norm_gain_vector, w_in, w_out)
    dlevel = lax.all_to_all(token_gradient, "var", split_axis=1, concat_axis=2, tiled=True)
    partial_grad = (
        jnp.einsum("bvnp,bne->vpe", patch_inputs, dlevel[:, 0], preferred_element_type=jnp.float32)
        * own_member[:, None, None]
    )
    kernel_grad = lax.psum_scatter(partial_grad, "dp", scatter_dimension=2, tiled=True) * scale
    return (block_out, kernel_grad)


def solution(mesh):
    placed = (
        P("dp", "var", None, None),
        P("var", None, None),
        P("var"),
        P(),
        P(),
        P(),
        P("dp", None, "var", None),
    )
    return jax.shard_map(
        local,
        mesh=mesh,
        in_specs=placed,
        out_specs=(P("dp", None, "var", None), P("var", None, "dp")),
        check_vma=False,
    )
```

profile of v0, /device:TPU:0, one launch (start us, length us, event | category | flops | bytes accessed | tf_op | source)
XLA Modules:
  0.0 89.8 jit_solution(14818469925672678726)
XLA Ops:
  7.2 0.0 copy-start
  7.2 0.0 copy-start.2
  7.2 1.4 %convert_reduce_fusion.1 = f32[]{:T(128)} fusion(s32[4]{0:T(128)} %param.9), kind=kLoop, calls=%fused_computation.48 | loop fusion | flops 7 | bytes 20 | tf_op jit(solution)/shard_map/reduce_sum | solution.py:53
  9.3 3.0 %reshape.106 = bf16[1,4,8,4,32,4]{5,4,3,2,1,0:T(8,128)(2,1)S(1)} reshape(bf16[1,4,32,128]{3,2,1,0:T(8,128)(2,1)} %param.7) | data formatting | bytes 65536 | tf_op jit(solution)/shard_map/reshape | solution.py:11
  12.3 0.0 copy-start.4
  12.3 0.9 copy.14
  13.2 0.1 reshape.107
  13.3 0.0 copy-done.2
  13.3 0.5 convolution_bitcast_fusion
  13.8 1.8 %copy.18 = bf16[4,256,512]{2,0,1:T(4,128)(2,1)} copy(bf16[4,256,512]{1,2,0:T(8,128)(2,1)S(1)} %convolution_bitcast_fusion) | data formatting | bytes 2097152 | tf_op jit(solution)/shard_map/reshape.3
  15.6 0.0 copy-done.4
  15.6 1.9 %fusion.47 = bf16[1,256,512]{2,0,1:T(2,128)(2,1)S(1)} fusion(bf16[4,256,512]{2,0,1:T(4,128)(2,1)} %copy.18, f32[]{:T(128)S(6)} %div.16, s32[4]{0:T(128)S(1)} %copy-done.4), kind=kOutput, calls=%fused_computation.62 | convolution fusion | flops 1048584 | bytes 1310740 | tf_op jit(solution)/shard_map/lv,bvne->blne/dot_general | solution.py:67
  17.6 0.0 copy-start.3
  17.6 0.4 copy.28
  18.0 0.5 broadcast.100
  18.5 2.3 %reduce.6 = bf16[256,512]{1,0:T(8,128)(2,1)S(1)} reduce(bf16[256,1,1,512]{3,2,1,0:T(2,128)(2,1)S(1)} %bitcast.92, bf16[]{:T(256)} %broadcast.100), dimensions={1,2}, to_apply=%bitcast.88.reduce_sub_computation | reduce | bytes 524290
  20.8 0.2 reshape.120
  21.0 10.7 %all_to_all.8 = bf16[4,2,16384]{2,1,0:T(2,128)(2,1)S(1)} all-to-all(bf16[4,2,16384]{2,1,0:T(2,128)(2,1)S(1)} %reshape.120), channel_id=1, replica_groups=mesh['var'=4,'dp'=8] {'var'}, dimensions={0} | all-to-all | bytes 524288 | tf_op jit(solution)/shard_map/all_to_all | solution.py:68
  31.7 0.3 reshape.121
  32.0 0.1 convert_reduce_fusion
  32.1 0.2 fusion.24
  32.3 0.0 copy-done
  32.3 0.0 copy-done.3
  32.3 0.0 copy-start.1
  32.3 2.1 %fusion.26 = f32[256,2048]{1,0:T(8,128)} fusion(bf16[512,2048]{1,0:T(8,128)(2,1)S(1)} %copy-done, bf16[1,1,256,512]{3,2,1,0:T(8,128)(2,1)S(1)} %get-tuple-element.5, f32[512]{0:T(512)S(1)} %copy-done.3, f32[256]{0:T(256)S(1)} %add_rsqrt_fusion, f32[256]{0:T(256)S(1)} %broadcast_multiply_fusion.3), kind=kOutput, calls=%fused_computation.35 | convolution fusion | flops 537526272 | bytes 4460544 | tf_op jit(solution)/shard_map/dot_general | solution.py:27
  34.5 0.0 copy-done.1
  34.5 4.7 %fusion.43 = (f32[256]{0:T(256)S(1)}, f32[256]{0:T(256)S(1)}, f32[256,512]{1,0:T(8,128)S(1)}) fusion(f32[256]{0:T(256)S(1)} %add_rsqrt_fusion, f32[256]{0:T(256)S(1)} %broadcast_multiply_fusion.3, bf16[1,1,256,512]{3,2,1,0:T(8,128)(2,1)S(1)} %get-tuple-element.5, f32[512]{0:T(512)S(1)} %copy-done.3, bf16[512,2048]{1,0:T(8,128)(2,1)S(1)} %copy-done, ...), kind=kOutput, calls=%fused_computation.59 | convolution fusion | flops 1085144576 | bytes 7346176 | tf_op jit(solution)/shard_map/dot_general | solution.py:36
  39.2 1.0 %fusion.22 = bf16[256,512]{1,0:T(8,128)(2,1)} fusion(bf16[1,1,256,512]{3,2,1,0:T(8,128)(2,1)S(1)} %get-tuple-element.5, f32[256,512]{1,0:T(8,128)S(1)} %get-tuple-element.6, f32[256]{0:T(256)S(1)} %get-tuple-element.7, f32[256]{0:T(256)S(1)} %get-tuple-element.8, f32[256]{0:T(256)S(1)} %add_rsqrt_fusion, f32[256]{0:T(256)S(1)} %broadcast_multiply_fusion.3, ...), kind=kLoop, calls=%fused_computation.30 | loop fusion | flops 1310720 | bytes 1314816 | tf_op jit(solution)/shard_map/convert_element_type | solution.py:45
  40.1 3.4 %all-to-all-start.1 = ((bf16[1,4,64,512]{3,2,0,1:T(8,128)(2,1)}), bf16[1,4,64,512]{3,2,0,1:T(8,128)(2,1)S(1)}, u32[]{:S(2)}, u32[]{:S(2)}) async-start(bf16[1,4,64,512]{3,2,0,1:T(8,128)(2,1)} %bitcast.11), calls=%async_computation.1 | async-start | bytes 524288 | tf_op jit(solution)/shard_map/all_to_all | solution.py:70
  43.5 0.0 reduce-scatter.4.cloned.1.call-start
  43.6 5.3 %all-to-all-done.1 = bf16[1,4,64,512]{3,2,0,1:T(8,128)(2,1)S(1)} async-done(((bf16[1,4,64,512]{3,2,0,1:T(8,128)(2,1)}), bf16[1,4,64,512]{3,2,0,1:T(8,128)(2,1)S(1)}, u32[]{:S(2)}, u32[]{:S(2)}) %all-to-all-start.1) | async-done | bytes 262176 | tf_op jit(solution)/shard_map/all_to_all | solution.py:70
  48.9 0.2 fusion.50
  49.0 0.1 multiply_bitcast_fusion
  49.1 0.4 copy.20
  49.5 1.2 %reshape.118 = f32[512,64]{1,0:T(8,128)} reshape(f32[512,4,16]{2,1,0:T(4,128)S(1)} %bitcast.89) | data formatting | bytes 262144
  50.7 0.0 reduce-scatter.4.cloned.1.call-update
  50.7 3.8 %fusion.7 = bf16[256,512]{1,0:T(8,128)(2,1)} fusion(bf16[2048,512]{1,0:T(8,128)(2,1)} %param.12, f32[256,2048]{1,0:T(8,128)} %fusion.26, bf16[1,1,256,512]{3,2,1,0:T(8,128)(2,1)S(1)} %get-tuple-element.5), kind=kOutput, calls=%fused_computation.13 | convolution fusion | flops 541982720 | bytes 4718592 | tf_op jit(solution)/shard_map/dot_general | solution.py:29
  54.5 26.9 %reduce-scatter.4.cloned.1.call-done = f32[64,64]{1,0:T(8,128)} async-done(((f32[512,64]{1,0:T(8,128)}), f32[64,64]{1,0:T(8,128)}) %reduce-scatter.4.cloned.1.call-update) | async-done | bytes 16400
  81.4 0.9 reshape.119
  82.3 0.1 copy.21
  82.3 0.6 broadcast_multiply_fusion
  (5 shorter events, 0.1 us)
Async XLA Ops:
  7.2 25.2 %copy-start = (bf16[512,2048]{1,0:T(8,128)(2,1)S(1)}, bf16[512,2048]{1,0:T(8,128)(2,1)}, u32[]{:S(2)}) copy-start(bf16[512,2048]{1,0:T(8,128)(2,1)} %param.11) | copy-start | bytes 6291460
  7.2 6.1 %copy-start.2 = (bf16[4,16,512]{2,1,0:T(8,128)(2,1)S(1)}, bf16[4,16,512]{2,1,0:T(8,128)(2,1)}, u32[]{:S(2)}) copy-start(bf16[4,16,512]{2,1,0:T(8,128)(2,1)} %param.8) | copy-start | bytes 196612
  12.3 3.3 %copy-start.4 = (s32[4]{0:T(128)S(1)}, s32[4]{0:T(128)}, u32[]{:S(2)}) copy-start(s32[4]{0:T(128)} %param.9) | copy-start | bytes 52
  17.6 14.7 %copy-start.3 = (f32[512]{0:T(512)S(1)}, f32[512]{0:T(512)}, u32[]{:S(2)}) copy-start(f32[512]{0:T(512)} %param.10) | copy-start | bytes 6148
  32.3 2.2 %copy-start.1 = (bf16[1,4,64,512]{3,2,1,0:T(8,128)(2,1)S(1)}, bf16[1,4,64,512]{3,2,1,0:T(8,128)(2,1)}, u32[]{:S(2)}) copy-start(bf16[1,4,64,512]{3,2,1,0:T(8,128)(2,1)} %param.13) | copy-start | bytes 786436
  40.1 8.8 %all-to-all-start.1 = ((bf16[1,4,64,512]{3,2,0,1:T(8,128)(2,1)}), bf16[1,4,64,512]{3,2,0,1:T(8,128)(2,1)S(1)}, u32[]{:S(2)}, u32[]{:S(2)}) async-start(bf16[1,4,64,512]{3,2,0,1:T(8,128)(2,1)} %bitcast.11), calls=%async_computation.1 | async-start | bytes 524288 | tf_op jit(solution)/shard_map/all_to_all | solution.py:70
  43.5 37.8 %reduce-scatter.4.cloned.1.call-start = ((), (), s32[]{:S(2)}) async-start(), calls=%async_computation.3 | async-start | bytes 294912
Sparse Core Ops, SparseCore 0:
  50.9 30.4 reduce-scatter.3
where the time goes:
time: 90.3 us; the launch traced here: 89.8 us
  waiting for transfers between devices  32.2 us (36%)
  between operations  14.9 us (17%)
  matrix products  13.1 us (15%)
  blocking collectives  10.7 us (12%)
  local copies, waits for them, and re-layouts  9.77 us (11%)
  other arithmetic  5.73 us (6%)
  starting transfers between devices  3.45 us (4%)
    unnamed x2, waiting for transfers between devices  26.9 us
    all_to_all x1, blocking collectives, local(): lax.all_to_all(token_rows, 'var', split_axis=2, concat_axis=1, tiled=True)  10.7 us
    all_to_all x1, waiting for transfers between devices, local(): lax.all_to_all(token_gradient, 'var', split_axis=1, concat_axis=2, tiled=...  5.28 us
    dot_general x1, matrix products, block_pass(): dnorm = jnp.dot(dpre, w_in.T, preferred_element_type=jnp.float32)  4.66 us
    dot_general x1, matrix products, block_pass(): jnp.dot(hidden, w_out, preferred_element_type=jnp.float32)  3.76 us
    unnamed x17, local copies, waits for them, and re-layouts  3.52 us
    all_to_all x1, starting transfers between devices, local(): lax.all_to_all(token_gradient, 'var', split_axis=1, concat_axis=2, tiled=...  3.41 us
    reshape x1, local copies, waits for them, and re-layouts, patches_of(): images.reshape(batch, count_v, height // PATCH, PATCH, width // PATCH, PA...  2.99 us
  transfers between devices with their start and end apart: 2, of which 2 were waited for; matrix products, arithmetic and copies ran while one was open for 4% of the time, Pallas kernels for 0%

commit v1 on v0

v1 whole, which is shorter than its diff:
```python
import functools

import jax
import jax.numpy as jnp
from jax import lax
from jax.experimental import pallas as pl
from jax.experimental.pallas import tpu as pltpu
from jax.sharding import PartitionSpec as P

PATCH = 4
LANES = 128
CHUNKS = 4
MESH = pl.DeviceIdType.MESH
F32 = jnp.float32
BF16 = jnp.bfloat16
GELU_C = 0.7978845608028654
GELU_A = 0.044715


def dot_nn(a, b):
    return lax.dot_general(a, b, (((1,), (0,)), ((), ())), preferred_element_type=F32)


def dot_nt(a, b):
    return lax.dot_general(a, b, (((1,), (1,)), ((), ())), preferred_element_type=F32)


def dot_tn(a, b):
    return lax.dot_general(a, b, (((0,), (0,)), ((), ())), preferred_element_type=F32)


def kernel(
    n_var, n_dp, width, scale, vars_local, wp, hp,
    map_ref, fields_hbm, kernels_hbm, gain_hbm, win_hbm, wout_hbm, cot_hbm,
    out_hbm, kg_ref,
    fields_v, kernels_v, gain_v, win, wout, cot_all, out_all,
    patch32, patch, gprime, gsend, grecv,
    in_sem, win_sem, wout_sem, cot_send, cot_recv, own_sem,
    out_send, out_recv, g_send, g_recv,
):
    my_var = lax.axis_index("var")
    my_dp = lax.axis_index("dp")
    features, hidden_units = win.shape
    step = hidden_units // CHUNKS
    rows = cot_all.shape[1]
    tokens_all = n_var * rows

    barrier = pltpu.get_barrier_semaphore()
    for k in range(1, n_var):
        pl.semaphore_signal(barrier, inc=1, device_id={"var": lax.rem(my_var + k, n_var)}, device_id_type=MESH)
    for k in range(1, n_dp):
        pl.semaphore_signal(barrier, inc=1, device_id={"dp": lax.rem(my_dp + k, n_dp)}, device_id_type=MESH)

    small = [
        pltpu.make_async_copy(fields_hbm, fields_v, in_sem.at[0]),
        pltpu.make_async_copy(kernels_hbm, kernels_v, in_sem.at[1]),
        pltpu.make_async_copy(gain_hbm, gain_v, in_sem.at[2]),
    ]
    for copy in small:
        copy.start()
    win_copies, wout_copies = [], []
    for c in range(CHUNKS):
        part = pl.ds(c * step, step)
        win_copies.append(pltpu.make_async_copy(win_hbm.at[:, part], win.at[:, part], win_sem.at[c]))
        wout_copies.append(pltpu.make_async_copy(wout_hbm.at[part], wout.at[part], wout_sem.at[c]))
        win_copies[c].start()
        wout_copies[c].start()

    pl.semaphore_wait(barrier, n_var - 1 + n_dp - 1)

    cot_copies = []
    for k in range(1, n_var):
        dest = lax.rem(my_var + k, n_var)
        cot_copies.append(pltpu.make_async_remote_copy(
            src_ref=cot_hbm.at[dest], dst_ref=cot_all.at[my_var],
            send_sem=cot_send.at[k], recv_sem=cot_recv.at[k],
            device_id={"var": dest}, device_id_type=MESH))
        cot_copies[-1].start()
    own_cot = pltpu.make_async_copy(cot_hbm.at[my_var], cot_all.at[my_var], own_sem.at[0])
    own_cot.start()

    small[0].wait()
    lines = fields_v.shape[0]
    group = LANES // wp
    per_hp = lines // hp
    r_id = lax.broadcasted_iota(jnp.int32, (LANES, LANES), 0)
    c_id = lax.broadcasted_iota(jnp.int32, (LANES, LANES), 1)
    pick = (r_id == PATCH * (c_id % wp) + c_id // wp).astype(BF16)
    o_id = lax.broadcasted_iota(jnp.int32, (lines, lines), 0)
    i_id = lax.broadcasted_iota(jnp.int32, (lines, lines), 1)
    order = (
        i_id == (hp * PATCH) * ((o_id // PATCH) % vars_local) + PATCH * (o_id // per_hp) + o_id % PATCH
    ).astype(BF16)
    spread = dot_nn(order, dot_nn(fields_v[...], pick).astype(BF16))
    lane_group = lax.broadcasted_iota(jnp.int32, (per_hp, LANES), 1) // wp
    for t in range(hp // group):
        for j in range(PATCH):
            block = None
            for g in range(group):
                source = spread[(group * t + g) * per_hp:(group * t + g + 1) * per_hp, :]
                shift = (wp * (g - j)) % LANES
                moved = pltpu.roll(source, shift, 1) if shift else source
                block = moved if block is None else jnp.where(lane_group == g, moved, block)
            patch32[t, pl.ds(j, per_hp, stride=PATCH), :] = block
        patch[:, t * LANES:(t + 1) * LANES] = patch32[t].astype(BF16)

    weights = [map_ref[v].astype(F32) for v in range(vars_local)]
    count = weights[0]
    for v in range(1, vars_local):
        count = count + weights[v]
    pp = PATCH * PATCH
    inv = 1.0 / jnp.maximum(jnp.full((1, features), count, F32), 1.0)
    row_var = lax.broadcasted_iota(jnp.int32, (vars_local * pp, 1), 0) // pp
    row_weight = jnp.zeros((vars_local * pp, 1), F32)
    for v in range(vars_local):
        row_weight = jnp.where(row_var == v, weights[v], row_weight)
    small[1].wait()
    chosen = (kernels_v[...].astype(F32) * row_weight).astype(BF16)
    tokens = (dot_tn(patch[...], chosen) * inv).astype(BF16).astype(F32)
    mean = jnp.mean(tokens, axis=1, keepdims=True)
    centered = tokens - mean
    rstd = lax.rsqrt(jnp.mean(centered * centered, axis=1, keepdims=True) + 1e-5)
    xhat = centered * rstd
    small[2].wait()
    gain = gain_v[...]
    normed = (xhat * gain).astype(BF16)

    total = tokens
    for c in range(CHUNKS):
        win_copies[c].wait()
        pre = dot_nn(normed, win[:, c * step:(c + 1) * step])
        sq = pre * pre
        half = 0.5 + 0.5 * jnp.tanh(pre * (GELU_C + (GELU_C * GELU_A) * sq))
        hid = pre * half
        gprime[:, c * step:(c + 1) * step] = half + hid * (1.0 - half) * (
            2.0 * GELU_C + (6.0 * GELU_C * GELU_A) * sq)
        wout_copies[c].wait()
        total = total + dot_nn(hid.astype(BF16), wout[c * step:(c + 1) * step, :])
    out_all[...] = total.astype(BF16).reshape(n_var, rows, features)

    out_copies = []
    for k in range(1, n_var):
        dest = lax.rem(my_var + k, n_var)
        out_copies.append(pltpu.make_async_remote_copy(
            src_ref=out_all.at[dest], dst_ref=out_hbm.at[my_var],
            send_sem=out_send.at[k], recv_sem=out_recv.at[k],
            device_id={"var": dest}, device_id_type=MESH))
        out_copies[-1].start()
    own_out = pltpu.make_async_copy(out_all.at[my_var], out_hbm.at[my_var], own_sem.at[1])
    own_out.start()

    own_cot.wait()
    for copy in cot_copies:
        copy.wait()
    cot = cot_all[...].reshape(tokens_all, features)
    dnorm = None
    for c in range(CHUNKS):
        dhid = dot_nt(cot, wout[c * step:(c + 1) * step, :])
        dpre = (dhid * gprime[:, c * step:(c + 1) * step]).astype(BF16)
        term = dot_nt(dpre, win[:, c * step:(c + 1) * step])
        dnorm = term if dnorm is None else dnorm + term
    dx = dnorm * gain
    dtok = cot.astype(F32) + rstd * (
        dx - jnp.mean(dx, axis=1, keepdims=True)
        - xhat * jnp.mean(dx * xhat, axis=1, keepdims=True))
    grad = dot_nn(patch[...], dtok.astype(BF16))

    per_tile = LANES // width
    short = grad.shape[0] // per_tile
    lane_part = lax.broadcasted_iota(jnp.int32, (short, LANES), 1) // width
    for d in range(n_dp):
        tile, j = d // per_tile, d % per_tile
        packed = None
        for g in range(per_tile):
            source = grad[g * short:(g + 1) * short, tile * LANES:(tile + 1) * LANES]
            shift = (width * (g - j)) % LANES
            moved = pltpu.roll(source, shift, 1) if shift else source
            packed = moved if packed is None else jnp.where(lane_part == g, moved, packed)
        gsend[d] = packed.astype(gsend.dtype)
    g_copies = []
    for k in range(1, n_dp):
        dest = lax.rem(my_dp + k, n_dp)
        g_copies.append(pltpu.make_async_remote_copy(
            src_ref=gsend.at[dest], dst_ref=grecv.at[k],
            send_sem=g_send.at[k], recv_sem=g_recv.at[k],
            device_id={"dp": dest}, device_id_type=MESH))
        g_copies[-1].start()
    own_out.wait()
    for copy in out_copies:
        copy.wait()
    summed = gsend[my_dp].astype(F32)
    for k in range(1, n_dp):
        g_copies[k - 1].wait_recv()
        summed = summed + grecv[k].astype(F32)
    factor = row_weight * (inv[:, :1] * scale)
    for g in range(per_tile):
        kg_ref[g * short:(g + 1) * short, :] = (
            summed[:, g * width:(g + 1) * width] * factor[g * short:(g + 1) * short])
    for copy in g_copies:
        copy.wait_send()


def local(n_var, n_dp, fields, kernels, level_map, norm_gain_vector, w_in, w_out, cotangent):
    batch, vars_local, height, across = fields.shape
    hp, wp = height // PATCH, across // PATCH
    features, hidden_units = w_in.shape
    levels, rows = cotangent.shape[1:3]
    width = features // n_dp
    scale = float(batch * n_dp * hp * wp) ** (-0.5)
    pp = PATCH * PATCH
    lines = vars_local * height
    short = vars_local * pp * width // LANES
    g_type = BF16 if short % 16 == 0 else F32
    tokens_all = hp * wp
    any_spec = pl.BlockSpec(memory_space=pl.ANY)
    dma = pltpu.SemaphoreType.DMA
    out, grad = pl.pallas_call(
        functools.partial(kernel, n_var, n_dp, width, scale, vars_local, wp, hp),
        out_shape=(
            jax.ShapeDtypeStruct((levels, rows, features), BF16),
            jax.ShapeDtypeStruct((vars_local * pp, width), F32),
        ),
        in_specs=[pl.BlockSpec(memory_space=pltpu.SMEM)] + [any_spec] * 6,
        out_specs=(any_spec, pl.BlockSpec(memory_space=pltpu.VMEM)),
        scratch_shapes=[
            pltpu.VMEM((lines, across), BF16),
            pltpu.VMEM((vars_local * pp, features), BF16),
            pltpu.VMEM((1, features), F32),
            pltpu.VMEM((features, hidden_units), BF16),
            pltpu.VMEM((hidden_units, features), BF16),
            pltpu.VMEM((n_var, rows, features), BF16),
            pltpu.VMEM((n_var, rows, features), BF16),
            pltpu.VMEM((tokens_all // LANES, vars_local * pp, LANES), F32),
            pltpu.VMEM((vars_local * pp, tokens_all), BF16),
            pltpu.VMEM((tokens_all, hidden_units), F32),
            pltpu.VMEM((n_dp, short, LANES), g_type),
            pltpu.VMEM((n_dp, short, LANES), g_type),
            dma((3,)), dma((CHUNKS,)), dma((CHUNKS,)),
            dma((n_var,)), dma((n_var,)), dma((2,)),
            dma((n_var,)), dma((n_var,)), dma((n_dp,)), dma((n_dp,)),
        ],
        compiler_params=pltpu.CompilerParams(
            collective_id=0, has_side_effects=True, vmem_limit_bytes=58 * 1024 * 1024),
    )(
        level_map,
        fields.reshape(lines, across),
        kernels.reshape(vars_local * pp, features),
        norm_gain_vector.reshape(1, features),
        w_in, w_out,
        cotangent.reshape(levels, rows, features),
    )
    return out.reshape(cotangent.shape), grad.reshape(vars_local, pp, width)


def solution(mesh):
    placed = (
        P("dp", "var", None, None),
        P("var", None, None),
        P("var"),
        P(),
        P(),
        P(),
        P("dp", None, "var", None),
    )
    return jax.shard_map(
        functools.partial(local, mesh.shape["var"], mesh.shape["dp"]),
        mesh=mesh,
        in_specs=placed,
        out_specs=(P("dp", None, "var", None), P("var", None, "dp")),
        check_vma=False,
    )
```

time: 90.3 us -> 20.8 us (0.23)
  waiting for transfers between devices: 32.2 us -> 0 us
  Pallas kernels: 0 us -> 16.9 us
  between operations: 14.9 us -> 0.64 us
  matrix products: 13.1 us -> 0 us
  blocking collectives: 10.7 us -> 0 us
  local copies, waits for them, and re-layouts: 9.77 us -> 3.04 us
  other arithmetic: 5.73 us -> 0 us
  starting transfers between devices: 3.45 us -> 0 us
    unnamed x2 -> x0, waiting for transfers between devices: 26.9 us -> none
    pallas_call x0 -> x1, Pallas kernels: none -> 16.9 us  [local(): pl.pallas_call(functools.partial(kernel, n_var, n_dp, width, scale, vars_...]
    dot_general x5 -> x0, matrix products: 12.9 us -> none  [the longest x1 4.66 us: block_pass(): dnorm = jnp.dot(dpre, w_in.T, preferred_element_type=jnp.float32)]
    all_to_all x1 -> x0, blocking collectives: 10.7 us -> none  [local(): lax.all_to_all(token_rows, 'var', split_axis=2, concat_axis=1, tiled=True)]
    all_to_all x1 -> x0, waiting for transfers between devices: 5.28 us -> none  [local(): lax.all_to_all(token_gradient, 'var', split_axis=1, concat_axis=2, tiled=...]
    all_to_all x1 -> x0, starting transfers between devices: 3.41 us -> none  [local(): lax.all_to_all(token_gradient, 'var', split_axis=1, concat_axis=2, tiled=...]
    reshape x2 -> x0, local copies, waits for them, and re-layouts: 3.13 us -> none  [the longest x1 2.99 us: patches_of(): images.reshape(batch, count_v, height // PATCH, PATCH, width // PATCH, PA...]
    unnamed x1 -> x0, other arithmetic: 2.27 us -> none
  transfers between devices with their start and end apart: 2 -> 0, of which waited for: 2 -> 0; matrix products, arithmetic and copies ran while one was open for 4% -> 0% of each run, Pallas kernels for 0% -> 0%
where the time goes in v1:
time: 20.8 us; the launch traced here: 20.6 us
  Pallas kernels  16.9 us (81%)
  local copies, waits for them, and re-layouts  3.04 us (15%)
  between operations  0.64 us (3%)
    pallas_call x1, Pallas kernels, local(): pl.pallas_call(functools.partial(kernel, n_var, n_dp, width, scale, vars_...  16.9 us
    unnamed x2, local copies, waits for them, and re-layouts  3.04 us

profile of v1, /device:TPU:0, one launch (start us, length us, event | category | flops | bytes accessed | tf_op | source)
XLA Modules:
  0.0 20.6 jit_solution(5815044809757224581)
XLA Ops:
  0.6 16.9 %shard_map.86 = (bf16[4,64,512]{2,1,0:T(8,128)(2,1)}, f32[64,64]{1,0:T(8,128)}) custom-call(s32[4]{0:T(128)} %map_ref.1, bf16[128,128]{1,0:T(8,128)(2,1)} %bitcast.9, bf16[64,512]{1,0:T(8,128)(2,1)} %bitcast.8, f32[1,512]{1,0:T(1,128)} %bitcast.11, bf16[512,2048]{1,0:T(8,128)(2,1)} %win_hbm.1, bf16[2048,512]{1,0:T(8,128)(2,1)} %wout_hbm.1, ...), custom_call_target="tpu_custom_call" | custom-call | tf_op jit(solution)/shard_map/pallas_call | solution.py:217
  17.5 1.7 %copy.11 = bf16[1,4,64,512]{3,2,1,0:T(8,128)(2,1)} copy(bf16[1,4,64,512]{3,2,1,0:T(8,128)(2,1)} %bitcast.7) | data formatting | bytes 524288
  19.2 1.4 %copy.12 = f32[4,16,64]{2,1,0:T(8,128)} copy(f32[4,16,64]{2,1,0:T(8,128)} %bitcast.10) | data formatting | bytes 32768

commit v2 on v1

--- a/solution.py
+++ b/solution.py
@@ -31,9 +31,9 @@
 
 def kernel(
     n_var, n_dp, width, scale, vars_local, wp, hp,
-    map_ref, fields_hbm, kernels_hbm, gain_hbm, win_hbm, wout_hbm, cot_hbm,
+    map_hbm, fields_hbm, kernels_hbm, gain_hbm, win_hbm, wout_hbm, cot_hbm,
     out_hbm, kg_ref,
-    fields_v, kernels_v, gain_v, win, wout, cot_all, out_all,
+    map_ref, fields_v, kernels_v, gain_v, win, wout, cot_all, out_all,
     patch32, patch, gprime, gsend, grecv,
     in_sem, win_sem, wout_sem, cot_send, cot_recv, own_sem,
     out_send, out_recv, g_send, g_recv,
@@ -55,6 +55,7 @@
         pltpu.make_async_copy(fields_hbm, fields_v, in_sem.at[0]),
         pltpu.make_async_copy(kernels_hbm, kernels_v, in_sem.at[1]),
         pltpu.make_async_copy(gain_hbm, gain_v, in_sem.at[2]),
+        pltpu.make_async_copy(map_hbm, map_ref, in_sem.at[3]),
     ]
     for copy in small:
         copy.start()
@@ -104,6 +105,7 @@
             patch32[t, pl.ds(j, per_hp, stride=PATCH), :] = block
         patch[:, t * LANES:(t + 1) * LANES] = patch32[t].astype(BF16)
 
+    small[3].wait()
     weights = [map_ref[v].astype(F32) for v in range(vars_local)]
     count = weights[0]
     for v in range(1, vars_local):
@@ -217,12 +219,13 @@
     out, grad = pl.pallas_call(
         functools.partial(kernel, n_var, n_dp, width, scale, vars_local, wp, hp),
         out_shape=(
-            jax.ShapeDtypeStruct((levels, rows, features), BF16),
-            jax.ShapeDtypeStruct((vars_local * pp, width), F32),
+            pltpu.VMEM((levels, rows, features), BF16),
+            pltpu.VMEM((vars_local * pp, width), F32),
         ),
-        in_specs=[pl.BlockSpec(memory_space=pltpu.SMEM)] + [any_spec] * 6,
+        in_specs=[any_spec] * 7,
         out_specs=(any_spec, pl.BlockSpec(memory_space=pltpu.VMEM)),
         scratch_shapes=[
+            pltpu.SMEM((vars_local,), jnp.int32),
             pltpu.VMEM((lines, across), BF16),
             pltpu.VMEM((vars_local * pp, features), BF16),
             pltpu.VMEM((1, features), F32),
@@ -235,7 +238,7 @@
             pltpu.VMEM((tokens_all, hidden_units), F32),
             pltpu.VMEM((n_dp, short, LANES), g_type),
             pltpu.VMEM((n_dp, short, LANES), g_type),
-            dma((3,)), dma((CHUNKS,)), dma((CHUNKS,)),
+            dma((4,)), dma((CHUNKS,)), dma((CHUNKS,)),
             dma((n_var,)), dma((n_var,)), dma((2,)),
             dma((n_var,)), dma((n_var,)), dma((n_dp,)), dma((n_dp,)),
         ],

time: 20.8 us -> 17.8 us (0.86)
  local copies, waits for them, and re-layouts: 3.04 us -> 1.32 us
  Pallas kernels: 16.9 us -> 15.6 us
    unnamed x2, local copies, waits for them, and re-layouts: 3.04 us -> 1.32 us
    pallas_call x1, Pallas kernels: 16.9 us -> 15.6 us  [local(): pl.pallas_call(functools.partial(kernel, n_var, n_dp, width, scale, vars_...]
where the time goes in v2:
time: 17.8 us; the launch traced here: 17.6 us
  Pallas kernels  15.6 us (88%)
  local copies, waits for them, and re-layouts  1.32 us (7%)
  between operations  0.64 us (4%)
    pallas_call x1, Pallas kernels, local(): pl.pallas_call(functools.partial(kernel, n_var, n_dp, width, scale, vars_...  15.6 us
    unnamed x2, local copies, waits for them, and re-layouts  1.32 us

profile of v2, /device:TPU:0, one launch (start us, length us, event | category | flops | bytes accessed | tf_op | source)
XLA Modules:
  0.0 17.6 jit_solution(6446312274080177738)
XLA Ops:
  0.6 15.6 %shard_map.86 = (bf16[4,64,512]{2,1,0:T(8,128)(2,1)S(1)}, f32[64,64]{1,0:T(8,128)S(1)}) custom-call(s32[4]{0:T(128)} %map_hbm.1, bf16[128,128]{1,0:T(8,128)(2,1)} %bitcast.10, bf16[64,512]{1,0:T(8,128)(2,1)} %bitcast.9, f32[1,512]{1,0:T(1,128)} %bitcast.11, bf16[512,2048]{1,0:T(8,128)(2,1)} %win_hbm.1, bf16[2048,512]{1,0:T(8,128)(2,1)} %wout_hbm.1, ...), custom_call_target="tpu_custom_call" | custom-call | tf_op jit(solution)/shard_map/pallas_call | solution.py:219
  16.3 0.7 %copy.11 = bf16[1,4,64,512]{3,2,1,0:T(8,128)(2,1)} copy(bf16[1,4,64,512]{3,2,1,0:T(8,128)(2,1)S(1)} %bitcast.6) | data formatting | bytes 524288
  17.0 0.6 %copy.12 = f32[4,16,64]{2,1,0:T(8,128)} copy(f32[4,16,64]{2,1,0:T(8,128)S(1)} %bitcast.7) | data formatting | bytes 32768

commit v3 on v2

--- a/solution.py
+++ b/solution.py
@@ -9,7 +9,7 @@
 
 PATCH = 4
 LANES = 128
-CHUNKS = 4
+CHUNKS = 1
 MESH = pl.DeviceIdType.MESH
 F32 = jnp.float32
 BF16 = jnp.bfloat16
@@ -127,16 +127,16 @@
     gain = gain_v[...]
     normed = (xhat * gain).astype(BF16)
 
+    for copy in win_copies + wout_copies:
+        copy.wait()
     total = tokens
     for c in range(CHUNKS):
-        win_copies[c].wait()
         pre = dot_nn(normed, win[:, c * step:(c + 1) * step])
         sq = pre * pre
         half = 0.5 + 0.5 * jnp.tanh(pre * (GELU_C + (GELU_C * GELU_A) * sq))
         hid = pre * half
         gprime[:, c * step:(c + 1) * step] = half + hid * (1.0 - half) * (
             2.0 * GELU_C + (6.0 * GELU_C * GELU_A) * sq)
-        wout_copies[c].wait()
         total = total + dot_nn(hid.astype(BF16), wout[c * step:(c + 1) * step, :])
     out_all[...] = total.astype(BF16).reshape(n_var, rows, features)
 

time: 17.8 us -> 17.5 us (0.983)
  Pallas kernels: 15.6 us -> 15.4 us
    pallas_call x1, Pallas kernels: 15.6 us -> 15.4 us  [local(): pl.pallas_call(functools.partial(kernel, n_var, n_dp, width, scale, vars_...]
where the time goes in v3:
time: 17.5 us; the launch traced here: 17.3 us
  Pallas kernels  15.4 us (88%)
  local copies, waits for them, and re-layouts  1.32 us (8%)
  between operations  0.64 us (4%)
    pallas_call x1, Pallas kernels, local(): pl.pallas_call(functools.partial(kernel, n_var, n_dp, width, scale, vars_...  15.4 us
    unnamed x2, local copies, waits for them, and re-layouts  1.32 us

profile of v3, /device:TPU:0, one launch (start us, length us, event | category | flops | bytes accessed | tf_op | source)
XLA Modules:
  0.0 17.3 jit_solution(10244245864892833340)
XLA Ops:
  0.6 15.4 %shard_map.86 = (bf16[4,64,512]{2,1,0:T(8,128)(2,1)S(1)}, f32[64,64]{1,0:T(8,128)S(1)}) custom-call(s32[4]{0:T(128)} %map_hbm.1, bf16[128,128]{1,0:T(8,128)(2,1)} %bitcast.10, bf16[64,512]{1,0:T(8,128)(2,1)} %bitcast.9, f32[1,512]{1,0:T(1,128)} %bitcast.11, bf16[512,2048]{1,0:T(8,128)(2,1)} %win_hbm.1, bf16[2048,512]{1,0:T(8,128)(2,1)} %wout_hbm.1, ...), custom_call_target="tpu_custom_call" | custom-call | tf_op jit(solution)/shard_map/pallas_call | solution.py:219
  16.0 0.7 %copy.11 = bf16[1,4,64,512]{3,2,1,0:T(8,128)(2,1)} copy(bf16[1,4,64,512]{3,2,1,0:T(8,128)(2,1)S(1)} %bitcast.6) | data formatting | bytes 524288
  16.7 0.6 %copy.12 = f32[4,16,64]{2,1,0:T(8,128)} copy(f32[4,16,64]{2,1,0:T(8,128)S(1)} %bitcast.7) | data formatting | bytes 32768
